TPU v7x, 512 devices: a whole 4x4x16 slice. The times are simulated.
512 devices in a mesh: net: 64 (over z, x), scen: 8 (over y, core).
Axes of the slice: x: 4, y: 4, z: 16, core: 2. Of those that a mesh axis runs over, the one named last changes fastest.
Arguments:
- device_group: int32 [64], replicated, may hold values from 3 to 63, as said below
- column_blocks: int32 [256, 12], P('net'), may hold values from 0 to 255, as said below
- impedance_real: bfloat16 [256, 12, 128, 128], P('net'), may hold values from 0 to 0.015258789
- impedance_imag: bfloat16 [256, 12, 128, 128], P('net'), may hold values from 0 to 0.0076293945
- building_phase: int32 [65536], P('net'), may hold values from 0 to 32767, as said below
- building_power: float32 [65536], P('net'), may hold values from 0.2 to 1
- reactive_ratio: float32 [65536], P('net'), may hold values from 0.1 to 0.8
- copula_normals: float32 [65536, 1024], P('net', 'scen'), may hold values from -6 to 6
- source_angle: float32 [32768], P('net'), may hold values from -3.140625 to 3.140625
Outputs:
- voltage_real: float32 [32768, 1024], P('net', 'scen')
- voltage_imag: float32 [32768, 1024], P('net', 'scen')
- drop_mean: float32 [32768, 16], P('net')
Inputs may be any that keep to these rules, and one draw needn't show every extreme that they name: `device_group`: never falling along the devices; each group is a run of 1 to 4 consecutive devices and is labelled by the index of its last device; the first 4 devices form one group. `column_blocks`: slot 0 of block row r is r itself; the first min(12, 4 times the devices of r's group) slots are distinct blocks of devices of r's group; the other slots repeat r. `building_phase`: building b feeds a phase of the device that holds b: from 512 * (b // 1024) to that plus 512 - 1; every phase is fed by at least one building.
All inputs are finite; a program needn't handle non-finite values.
Results may differ from a plain program's by a relative error of at most 0.0063.
Values may be sent and summed in bfloat16 or wider, within the bound.
No kernel may reach another device: no remote copies, remote signals or barrier semaphores. Data moves between devices by JAX's collectives and lax.ppermute only.
A program may use at most 64 MiB of HBM per device.

v0:
```python
import jax
import jax.numpy as jnp
from jax import lax
from jax.sharding import PartitionSpec as P

GMAX = 4
ITERS = 3
TIMES = 16
floor_square = 0.49


def from_behind(value, axis, steps):
    count = lax.axis_size(axis)
    leading, last = (max(0, -steps), min(count, count - steps))
    return lax.ppermute(value, axis, [(source, source + steps) for source in range(leading, last)])


def shards(
    device_group,
    column_blocks,
    impedance_real,
    impedance_imag,
    building_phase,
    building_power,
    reactive_ratio,
    copula_normals,
    source_angle,
):
    block_count, slot_count, block_width, other_width = impedance_real.shape
    phase_count = block_count * block_width
    column_count = copula_normals.shape[1]
    local_scen = column_count // TIMES
    total_scen = local_scen * lax.axis_size("scen")
    scenario = (
        lax.axis_index("scen") * local_scen + jnp.arange(column_count, dtype=jnp.int32) // TIMES
    ).astype(jnp.float32)
    scen_level = 0.5 + scenario / (total_scen - 1)
    real_power = (
        building_power[:, None] * scen_level[None, :] * jnp.exp(0.4 * copula_normals - 0.08)
    )
    both_power = jnp.concatenate([real_power, real_power * reactive_ratio[:, None]], axis=1)
    net_index = lax.axis_index("net")
    local_phase = building_phase - net_index * phase_count
    loads = jax.ops.segment_sum(both_power, local_phase, num_segments=phase_count)
    load_real = loads[:, :column_count]
    load_reactive = loads[:, column_count:]
    source_real = jnp.broadcast_to(jnp.cos(source_angle)[:, None], (phase_count, column_count))
    source_imag = jnp.broadcast_to(jnp.sin(source_angle)[:, None], (phase_count, column_count))
    own_group = device_group[net_index]
    group_size = jnp.sum((device_group == own_group).astype(jnp.int32))
    live_count = jnp.minimum(slot_count, group_size * block_count)
    live_slots = jnp.arange(slot_count, dtype=jnp.int32) < live_count
    owner_device = column_blocks // block_count
    window_index = (
        owner_device - net_index + (GMAX - 1)
    ) * block_count + column_blocks % block_count
    volt_real = source_real
    volt_imag = source_imag
    for sweep in range(ITERS):
        mag_square = jnp.maximum(volt_real * volt_real + volt_imag * volt_imag, floor_square)
        current_real = (load_real * volt_real + load_reactive * volt_imag) / mag_square
        current_imag = (load_real * volt_imag - load_reactive * volt_real) / mag_square
        currents = jnp.concatenate([current_real, current_imag], axis=1).astype(jnp.bfloat16)
        lower_parts = []
        upper_parts = []
        for distance in range(1, GMAX):
            lower_parts.append(from_behind(currents, "net", distance))
            upper_parts.append(from_behind(currents, "net", -distance))
        nearby = jnp.concatenate(lower_parts[::-1] + [currents] + upper_parts, axis=0).reshape(
            -1, block_width, 2 * column_count
        )
        gathered = jnp.take(nearby, window_index, axis=0)
        gathered = jnp.where(live_slots[None, :, None, None], gathered, jnp.zeros((), jnp.bfloat16))
        real_part = jnp.einsum(
            "bsij,bsjk->bik", impedance_real, gathered, preferred_element_type=jnp.float32
        ).reshape(phase_count, 2 * column_count)
        imag_part = jnp.einsum(
            "bsij,bsjk->bik", impedance_imag, gathered, preferred_element_type=jnp.float32
        ).reshape(phase_count, 2 * column_count)
        drop_real = real_part[:, :column_count] - imag_part[:, column_count:]
        drop_imag = real_part[:, column_count:] + imag_part[:, :column_count]
        volt_real = source_real - drop_real
        volt_imag = source_imag - drop_imag
    magnitude = jnp.sqrt(volt_real * volt_real + volt_imag * volt_imag)
    local_sum = jnp.sum(magnitude.reshape(phase_count, local_scen, TIMES), axis=1)
    scen_total = lax.psum(local_sum, "scen")
    drop_mean = 100.0 * (1.0 - scen_total / total_scen)
    return (volt_real, volt_imag, drop_mean)


def solution(mesh):
    in_specs = (
        P(),
        P("net", None),
        P("net", None, None, None),
        P("net", None, None, None),
        P("net"),
        P("net"),
        P("net"),
        P("net", "scen"),
        P("net"),
    )
    out_specs = (P("net", "scen"), P("net", "scen"), P("net", None))
    return jax.shard_map(shards, mesh=mesh, in_specs=in_specs, out_specs=out_specs, check_vma=False)
```

profile of v0, /device:TPU:224, one launch (start us, length us, event | category | flops | bytes accessed | tf_op | source)
XLA Modules:
  0.0 170.0 jit_solution(13973513056029608391)
XLA Ops:
  3.6 6.2 %scatter_custom_fusion = f32[512,256]{1,0:T(8,128)S(1)} fusion(s32[1024]{0:T(1024)S(1)} %broadcast_subtract_fusion, f32[1024,128]{1,0:T(8,128)S(1)} %get-tuple-element.12, f32[]{:T(128)} %constant.112, f32[1024,128]{1,0:T(8,128)S(1)} %get-tuple-element.13, f32[]{:T(128)} %constant.78.clone.1), kind=kCustom, calls=%fused_computation.7 | custom fusion | flops 524288 | bytes 1572872 | tf_op jit(solution)/shard_map/scatter-add | solution.py:44
  10.2 4.7 %collective-permute-start = (bf16[512,256]{1,0:T(8,128)(2,1)S(1)}, bf16[512,256]{1,0:T(8,128)(2,1)}, u32[]{:S(2)}, u32[]{:S(2)}) collective-permute-start(bf16[512,256]{1,0:T(8,128)(2,1)S(1)} %pad_maximum_fusion), channel_id=1, source_target_pairs={{0,24},{8,32},{16,40},{24,48},{32,56},{40,64},{48,72},{56,80},{64,... | collective-permute-start | bytes 786440 | tf_op jit(solution)/shard_map/ppermute | solution.py:15
  14.9 5.3 %collective-permute-start.1 = (bf16[512,256]{1,0:T(8,128)(2,1)S(1)}, bf16[512,256]{1,0:T(8,128)(2,1)}, u32[]{:S(2)}, u32[]{:S(2)}) collective-permute-start(bf16[512,256]{1,0:T(8,128)(2,1)S(1)} %pad_maximum_fusion), channel_id=1, source_target_pairs={{0,16},{8,24},{16,32},{24,40},{32,48},{40,56},{48,64},{56,72},{64,... | collective-permute-start | bytes 786440 | tf_op jit(solution)/shard_map/ppermute | solution.py:15
  20.1 2.8 %collective-permute-start.2 = (bf16[512,256]{1,0:T(8,128)(2,1)S(1)}, bf16[512,256]{1,0:T(8,128)(2,1)S(1)}, u32[]{:S(2)}, u32[]{:S(2)}) collective-permute-start(bf16[512,256]{1,0:T(8,128)(2,1)S(1)} %pad_maximum_fusion), channel_id=1, source_target_pairs={{0,8},{8,16},{16,24},{24,32},{32,40},{40,48},{48,56},{56,64},{64,7... | collective-permute-start | bytes 786440 | tf_op jit(solution)/shard_map/ppermute | solution.py:15
  22.9 5.2 %collective-permute-start.3 = (bf16[512,256]{1,0:T(8,128)(2,1)S(1)}, bf16[512,256]{1,0:T(8,128)(2,1)S(1)}, u32[]{:S(2)}, u32[]{:S(2)}) collective-permute-start(bf16[512,256]{1,0:T(8,128)(2,1)S(1)} %pad_maximum_fusion), channel_id=1, source_target_pairs={{8,0},{16,8},{24,16},{32,24},{40,32},{48,40},{56,48},{64,56},{72,6... | collective-permute-start | bytes 786440 | tf_op jit(solution)/shard_map/ppermute | solution.py:15
  28.1 1.9 %collective-permute-start.4 = (bf16[512,256]{1,0:T(8,128)(2,1)S(1)}, bf16[512,256]{1,0:T(8,128)(2,1)S(1)}, u32[]{:S(2)}, u32[]{:S(2)}) collective-permute-start(bf16[512,256]{1,0:T(8,128)(2,1)S(1)} %pad_maximum_fusion), channel_id=1, source_target_pairs={{16,0},{24,8},{32,16},{40,24},{48,32},{56,40},{64,48},{72,56},{80,... | collective-permute-start | bytes 786440 | tf_op jit(solution)/shard_map/ppermute | solution.py:15
  32.7 1.9 %collective-permute-start.5 = (bf16[512,256]{1,0:T(8,128)(2,1)S(1)}, bf16[512,256]{1,0:T(8,128)(2,1)S(1)}, u32[]{:S(2)}, u32[]{:S(2)}) collective-permute-start(bf16[512,256]{1,0:T(8,128)(2,1)S(1)} %pad_maximum_fusion), channel_id=1, source_target_pairs={{24,0},{32,8},{40,16},{48,24},{56,32},{64,40},{72,48},{80,56},{88,... | collective-permute-start | bytes 786440 | tf_op jit(solution)/shard_map/ppermute | solution.py:15
  40.2 5.0 %collective-permute-done.4 = bf16[512,256]{1,0:T(8,128)(2,1)S(1)} collective-permute-done((bf16[512,256]{1,0:T(8,128)(2,1)S(1)}, bf16[512,256]{1,0:T(8,128)(2,1)S(1)}, u32[]{:S(2)}, u32[]{:S(2)}) %collective-permute-start.4) | collective-permute-done | bytes 262176 | tf_op jit(solution)/shard_map/ppermute | solution.py:15
  46.7 4.0 %gather_fusion = bf16[48,128,256]{2,1,0:T(8,128)(2,1)} fusion(bf16[28,128,256]{2,1,0:T(8,128)(2,1)} %bitcast.1, s32[1024]{0:T(1024)S(1)} %pad_clamp_fusion), kind=kCustom, calls=%fused_computation.clone | custom fusion | bytes 6291648 | tf_op jit(solution)/shard_map/jit(_take)/gather | solution.py:72
  50.7 2.8 %fusion.4 = f32[4,256,128,1]{1,2,3,0:T(8,128)S(1)} fusion(bf16[4,12,128,128]{3,2,1,0:T(8,128)(2,1)S(1)} %copy-done, bf16[4,12,128,256]{3,2,1,0:T(8,128)(2,1)} %bitcast.53, pred[12]{0:T(512)(128)(4,1)S(1)} %iota_compare_fusion, pred[4,12]{1,0:T(4,128)(4,1)S(1)} %get-tuple-element.10), kind=kOutput, calls=%fused_computation.11 | convolution fusion | flops 405798912 | bytes 5242940 | tf_op jit(solution)/shard_map/bsij,bsjk->bik/dot_general | solution.py:74
  57.0 10.6 %collective-permute-start.7 = (bf16[512,256]{1,0:T(8,128)(2,1)S(1)}, bf16[512,256]{1,0:T(8,128)(2,1)S(1)}, u32[]{:S(2)}, u32[]{:S(2)}) collective-permute-start(bf16[512,256]{1,0:T(8,128)(2,1)S(1)} %pad_maximum_fusion.1), channel_id=1, source_target_pairs={{0,16},{8,24},{16,32},{24,40},{32,48},{40,56},{48,64},{56,72},{64,... | collective-permute-start | bytes 786440 | tf_op jit(solution)/shard_map/ppermute | solution.py:15
  69.5 6.0 %collective-permute-start.9 = (bf16[512,256]{1,0:T(8,128)(2,1)S(1)}, bf16[512,256]{1,0:T(8,128)(2,1)S(1)}, u32[]{:S(2)}, u32[]{:S(2)}) collective-permute-start(bf16[512,256]{1,0:T(8,128)(2,1)S(1)} %pad_maximum_fusion.1), channel_id=1, source_target_pairs={{8,0},{16,8},{24,16},{32,24},{40,32},{48,40},{56,48},{64,56},{72,6... | collective-permute-start | bytes 786440 | tf_op jit(solution)/shard_map/ppermute | solution.py:15
  83.1 7.1 %collective-permute-done.10 = bf16[512,256]{1,0:T(8,128)(2,1)S(1)} collective-permute-done((bf16[512,256]{1,0:T(8,128)(2,1)S(1)}, bf16[512,256]{1,0:T(8,128)(2,1)S(1)}, u32[]{:S(2)}, u32[]{:S(2)}) %collective-permute-start.10) | collective-permute-done | bytes 262176 | tf_op jit(solution)/shard_map/ppermute | solution.py:15
  91.7 4.0 %gather_fusion.1 = bf16[48,128,256]{2,1,0:T(8,128)(2,1)} fusion(bf16[28,128,256]{2,1,0:T(8,128)(2,1)} %bitcast.15, s32[1024]{0:T(1024)S(1)} %pad_clamp_fusion), kind=kCustom, calls=%fused_computation.1.clone | custom fusion | bytes 6291648 | tf_op jit(solution)/shard_map/jit(_take)/gather | solution.py:72
  95.7 2.8 %fusion.6 = f32[4,256,128,1]{1,2,3,0:T(8,128)S(1)} fusion(bf16[4,12,128,128]{3,2,1,0:T(8,128)(2,1)S(1)} %copy-done, bf16[4,12,128,256]{3,2,1,0:T(8,128)(2,1)} %bitcast.55, pred[12]{0:T(512)(128)(4,1)S(1)} %iota_compare_fusion, pred[4,12]{1,0:T(4,128)(4,1)S(1)} %get-tuple-element.10), kind=kOutput, calls=%fused_computation.13 | convolution fusion | flops 405798912 | bytes 5242940 | tf_op jit(solution)/shard_map/bsij,bsjk->bik/dot_general | solution.py:74
  102.0 5.8 %collective-permute-start.13 = (bf16[512,256]{1,0:T(8,128)(2,1)S(1)}, bf16[512,256]{1,0:T(8,128)(2,1)S(1)}, u32[]{:S(2)}, u32[]{:S(2)}) collective-permute-start(bf16[512,256]{1,0:T(8,128)(2,1)S(1)} %pad_maximum_fusion.2), channel_id=1, source_target_pairs={{0,16},{8,24},{16,32},{24,40},{32,48},{40,56},{48,64},{56,72},{64,... | collective-permute-start | bytes 786440 | tf_op jit(solution)/shard_map/ppermute | solution.py:15
  107.8 3.5 %collective-permute-start.14 = (bf16[512,256]{1,0:T(8,128)(2,1)S(1)}, bf16[512,256]{1,0:T(8,128)(2,1)S(1)}, u32[]{:S(2)}, u32[]{:S(2)}) collective-permute-start(bf16[512,256]{1,0:T(8,128)(2,1)S(1)} %pad_maximum_fusion.2), channel_id=1, source_target_pairs={{0,8},{8,16},{16,24},{24,32},{32,40},{40,48},{48,56},{56,64},{64,7... | collective-permute-start | bytes 786440 | tf_op jit(solution)/shard_map/ppermute | solution.py:15
  111.3 5.5 %collective-permute-start.15 = (bf16[512,256]{1,0:T(8,128)(2,1)S(1)}, bf16[512,256]{1,0:T(8,128)(2,1)S(1)}, u32[]{:S(2)}, u32[]{:S(2)}) collective-permute-start(bf16[512,256]{1,0:T(8,128)(2,1)S(1)} %pad_maximum_fusion.2), channel_id=1, source_target_pairs={{8,0},{16,8},{24,16},{32,24},{40,32},{48,40},{56,48},{64,56},{72,6... | collective-permute-start | bytes 786440 | tf_op jit(solution)/shard_map/ppermute | solution.py:15
  116.8 3.4 %collective-permute-start.16 = (bf16[512,256]{1,0:T(8,128)(2,1)S(1)}, bf16[512,256]{1,0:T(8,128)(2,1)S(1)}, u32[]{:S(2)}, u32[]{:S(2)}) collective-permute-start(bf16[512,256]{1,0:T(8,128)(2,1)S(1)} %pad_maximum_fusion.2), channel_id=1, source_target_pairs={{16,0},{24,8},{32,16},{40,24},{48,32},{56,40},{64,48},{72,56},{80,... | collective-permute-start | bytes 786440 | tf_op jit(solution)/shard_map/ppermute | solution.py:15
  122.2 4.5 %collective-permute-done.14 = bf16[512,256]{1,0:T(8,128)(2,1)S(1)} collective-permute-done((bf16[512,256]{1,0:T(8,128)(2,1)S(1)}, bf16[512,256]{1,0:T(8,128)(2,1)S(1)}, u32[]{:S(2)}, u32[]{:S(2)}) %collective-permute-start.14) | collective-permute-done | bytes 262176 | tf_op jit(solution)/shard_map/ppermute | solution.py:15
  126.7 7.5 %collective-permute-done.16 = bf16[512,256]{1,0:T(8,128)(2,1)S(1)} collective-permute-done((bf16[512,256]{1,0:T(8,128)(2,1)S(1)}, bf16[512,256]{1,0:T(8,128)(2,1)S(1)}, u32[]{:S(2)}, u32[]{:S(2)}) %collective-permute-start.16) | collective-permute-done | bytes 262176 | tf_op jit(solution)/shard_map/ppermute | solution.py:15
  135.8 2.5 %gather_fusion.2 = bf16[48,128,256]{2,1,0:T(8,128)(2,1)} fusion(bf16[28,128,256]{2,1,0:T(8,128)(2,1)S(1)} %bitcast.50, s32[1024]{0:T(1024)S(1)} %pad_clamp_fusion), kind=kCustom, calls=%fused_computation.2.clone | custom fusion | bytes 6291648 | tf_op jit(solution)/shard_map/jit(_take)/gather | solution.py:72
  138.3 2.8 %fusion.8 = f32[4,256,128,1]{1,2,3,0:T(8,128)S(1)} fusion(bf16[4,12,128,128]{3,2,1,0:T(8,128)(2,1)S(1)} %copy-done, bf16[4,12,128,256]{3,2,1,0:T(8,128)(2,1)} %bitcast.51, pred[12]{0:T(512)(128)(4,1)S(1)} %iota_compare_fusion, pred[4,12]{1,0:T(4,128)(4,1)S(1)} %get-tuple-element.10), kind=kOutput, calls=%fused_computation.15 | convolution fusion | flops 405798912 | bytes 5242940 | tf_op jit(solution)/shard_map/bsij,bsjk->bik/dot_general | solution.py:74
  143.6 25.8 %psum.7 = f32[512,16]{0,1:T(8,128)S(1)} all-reduce(f32[512,16]{0,1:T(8,128)S(1)} %reduce_sum.19), channel_id=1, replica_groups=mesh['net'=64,'scen'=8] {'scen'}, use_global_device_ids=true, to_apply=%region_3.5 | all-reduce | flops 8192 | bytes 65536 | tf_op jit(solution)/shard_map/psum | solution.py:86
  (83 shorter events, 36.6 us)
Async XLA Ops:
  0.6 50.0 %copy-start = (bf16[4,12,128,128]{3,2,1,0:T(8,128)(2,1)S(1)}, bf16[4,12,128,128]{3,2,1,0:T(8,128)(2,1)}, u32[]{:S(2)}) copy-start(bf16[4,12,128,128]{3,2,1,0:T(8,128)(2,1)} %param.13) | copy-start | bytes 4718596
  3.6 26.5 %copy-start.4 = (s32[4,12]{1,0:T(4,128)S(1)}, s32[4,12]{1,0:T(4,128)}, u32[]{:S(2)}) copy-start(s32[4,12]{1,0:T(4,128)} %param.12) | copy-start | bytes 580
  3.6 26.6 %copy-start.8 = (s32[64]{0:T(128)S(1)}, s32[64]{0:T(128)}, u32[]{:S(2)}) copy-start(s32[64]{0:T(128)} %param.11) | copy-start | bytes 772
  10.2 22.5 %collective-permute-start = (bf16[512,256]{1,0:T(8,128)(2,1)S(1)}, bf16[512,256]{1,0:T(8,128)(2,1)}, u32[]{:S(2)}, u32[]{:S(2)}) collective-permute-start(bf16[512,256]{1,0:T(8,128)(2,1)S(1)} %pad_maximum_fusion), channel_id=1, source_target_pairs={{0,24},{8,32},{16,40},{24,48},{32,56},{40,64},{48,72},{56,80},{64,... | collective-permute-start | bytes 786440 | tf_op jit(solution)/shard_map/ppermute | solution.py:15
  14.9 21.4 %collective-permute-start.1 = (bf16[512,256]{1,0:T(8,128)(2,1)S(1)}, bf16[512,256]{1,0:T(8,128)(2,1)}, u32[]{:S(2)}, u32[]{:S(2)}) collective-permute-start(bf16[512,256]{1,0:T(8,128)(2,1)S(1)} %pad_maximum_fusion), channel_id=1, source_target_pairs={{0,16},{8,24},{16,32},{24,40},{32,48},{40,56},{48,64},{56,72},{64,... | collective-permute-start | bytes 786440 | tf_op jit(solution)/shard_map/ppermute | solution.py:15
  20.1 17.8 %collective-permute-start.2 = (bf16[512,256]{1,0:T(8,128)(2,1)S(1)}, bf16[512,256]{1,0:T(8,128)(2,1)S(1)}, u32[]{:S(2)}, u32[]{:S(2)}) collective-permute-start(bf16[512,256]{1,0:T(8,128)(2,1)S(1)} %pad_maximum_fusion), channel_id=1, source_target_pairs={{0,8},{8,16},{16,24},{24,32},{32,40},{40,48},{48,56},{56,64},{64,7... | collective-permute-start | bytes 786440 | tf_op jit(solution)/shard_map/ppermute | solution.py:15
  22.9 16.5 %collective-permute-start.3 = (bf16[512,256]{1,0:T(8,128)(2,1)S(1)}, bf16[512,256]{1,0:T(8,128)(2,1)S(1)}, u32[]{:S(2)}, u32[]{:S(2)}) collective-permute-start(bf16[512,256]{1,0:T(8,128)(2,1)S(1)} %pad_maximum_fusion), channel_id=1, source_target_pairs={{8,0},{16,8},{24,16},{32,24},{40,32},{48,40},{56,48},{64,56},{72,6... | collective-permute-start | bytes 786440 | tf_op jit(solution)/shard_map/ppermute | solution.py:15
  28.1 17.1 %collective-permute-start.4 = (bf16[512,256]{1,0:T(8,128)(2,1)S(1)}, bf16[512,256]{1,0:T(8,128)(2,1)S(1)}, u32[]{:S(2)}, u32[]{:S(2)}) collective-permute-start(bf16[512,256]{1,0:T(8,128)(2,1)S(1)} %pad_maximum_fusion), channel_id=1, source_target_pairs={{16,0},{24,8},{32,16},{40,24},{48,32},{56,40},{64,48},{72,56},{80,... | collective-permute-start | bytes 786440 | tf_op jit(solution)/shard_map/ppermute | solution.py:15
  32.7 13.2 %collective-permute-start.5 = (bf16[512,256]{1,0:T(8,128)(2,1)S(1)}, bf16[512,256]{1,0:T(8,128)(2,1)S(1)}, u32[]{:S(2)}, u32[]{:S(2)}) collective-permute-start(bf16[512,256]{1,0:T(8,128)(2,1)S(1)} %pad_maximum_fusion), channel_id=1, source_target_pairs={{24,0},{32,8},{40,16},{48,24},{56,32},{64,40},{72,48},{80,56},{88,... | collective-permute-start | bytes 786440 | tf_op jit(solution)/shard_map/ppermute | solution.py:15
  50.7 3.3 %copy-start.5 = (bf16[4,12,128,128]{3,2,1,0:T(8,128)(2,1)S(1)}, bf16[4,12,128,128]{3,2,1,0:T(8,128)(2,1)}, u32[]{:S(2)}) copy-start(bf16[4,12,128,128]{3,2,1,0:T(8,128)(2,1)} %param.14) | copy-start | bytes 4718596
  55.0 22.4 %collective-permute-start.6 = (bf16[512,256]{1,0:T(8,128)(2,1)S(1)}, bf16[512,256]{1,0:T(8,128)(2,1)S(1)}, u32[]{:S(2)}, u32[]{:S(2)}) collective-permute-start(bf16[512,256]{1,0:T(8,128)(2,1)S(1)} %pad_maximum_fusion.1), channel_id=1, source_target_pairs={{0,24},{8,32},{16,40},{24,48},{32,56},{40,64},{48,72},{56,80},{64,... | collective-permute-start | bytes 786440 | tf_op jit(solution)/shard_map/ppermute | solution.py:15
  57.0 23.1 %collective-permute-start.7 = (bf16[512,256]{1,0:T(8,128)(2,1)S(1)}, bf16[512,256]{1,0:T(8,128)(2,1)S(1)}, u32[]{:S(2)}, u32[]{:S(2)}) collective-permute-start(bf16[512,256]{1,0:T(8,128)(2,1)S(1)} %pad_maximum_fusion.1), channel_id=1, source_target_pairs={{0,16},{8,24},{16,32},{24,40},{32,48},{40,56},{48,64},{56,72},{64,... | collective-permute-start | bytes 786440 | tf_op jit(solution)/shard_map/ppermute | solution.py:15
  67.6 13.3 %collective-permute-start.8 = (bf16[512,256]{1,0:T(8,128)(2,1)S(1)}, bf16[512,256]{1,0:T(8,128)(2,1)S(1)}, u32[]{:S(2)}, u32[]{:S(2)}) collective-permute-start(bf16[512,256]{1,0:T(8,128)(2,1)S(1)} %pad_maximum_fusion.1), channel_id=1, source_target_pairs={{0,8},{8,16},{16,24},{24,32},{32,40},{40,48},{48,56},{56,64},{64,7... | collective-permute-start | bytes 786440 | tf_op jit(solution)/shard_map/ppermute | solution.py:15
  69.5 12.8 %collective-permute-start.9 = (bf16[512,256]{1,0:T(8,128)(2,1)S(1)}, bf16[512,256]{1,0:T(8,128)(2,1)S(1)}, u32[]{:S(2)}, u32[]{:S(2)}) collective-permute-start(bf16[512,256]{1,0:T(8,128)(2,1)S(1)} %pad_maximum_fusion.1), channel_id=1, source_target_pairs={{8,0},{16,8},{24,16},{32,24},{40,32},{48,40},{56,48},{64,56},{72,6... | collective-permute-start | bytes 786440 | tf_op jit(solution)/shard_map/ppermute | solution.py:15
  75.5 14.6 %collective-permute-start.10 = (bf16[512,256]{1,0:T(8,128)(2,1)S(1)}, bf16[512,256]{1,0:T(8,128)(2,1)S(1)}, u32[]{:S(2)}, u32[]{:S(2)}) collective-permute-start(bf16[512,256]{1,0:T(8,128)(2,1)S(1)} %pad_maximum_fusion.1), channel_id=1, source_target_pairs={{16,0},{24,8},{32,16},{40,24},{48,32},{56,40},{64,48},{72,56},{80,... | collective-permute-start | bytes 786440 | tf_op jit(solution)/shard_map/ppermute | solution.py:15
  77.5 13.5 %collective-permute-start.11 = (bf16[512,256]{1,0:T(8,128)(2,1)S(1)}, bf16[512,256]{1,0:T(8,128)(2,1)S(1)}, u32[]{:S(2)}, u32[]{:S(2)}) collective-permute-start(bf16[512,256]{1,0:T(8,128)(2,1)S(1)} %pad_maximum_fusion.1), channel_id=1, source_target_pairs={{24,0},{32,8},{40,16},{48,24},{56,32},{64,40},{72,48},{80,56},{88,... | collective-permute-start | bytes 786440 | tf_op jit(solution)/shard_map/ppermute | solution.py:15
  95.7 3.3 %copy-start.6 = (bf16[4,12,128,128]{3,2,1,0:T(8,128)(2,1)S(1)}, bf16[4,12,128,128]{3,2,1,0:T(8,128)(2,1)}, u32[]{:S(2)}) copy-start(bf16[4,12,128,128]{3,2,1,0:T(8,128)(2,1)} %param.14) | copy-start | bytes 4718596
  100.1 20.1 %collective-permute-start.12 = (bf16[512,256]{1,0:T(8,128)(2,1)S(1)}, bf16[512,256]{1,0:T(8,128)(2,1)S(1)}, u32[]{:S(2)}, u32[]{:S(2)}) collective-permute-start(bf16[512,256]{1,0:T(8,128)(2,1)S(1)} %pad_maximum_fusion.2), channel_id=1, source_target_pairs={{0,24},{8,32},{16,40},{24,48},{32,56},{40,64},{48,72},{56,80},{64,... | collective-permute-start | bytes 786440 | tf_op jit(solution)/shard_map/ppermute | solution.py:15
  102.0 20.2 %collective-permute-start.13 = (bf16[512,256]{1,0:T(8,128)(2,1)S(1)}, bf16[512,256]{1,0:T(8,128)(2,1)S(1)}, u32[]{:S(2)}, u32[]{:S(2)}) collective-permute-start(bf16[512,256]{1,0:T(8,128)(2,1)S(1)} %pad_maximum_fusion.2), channel_id=1, source_target_pairs={{0,16},{8,24},{16,32},{24,40},{32,48},{40,56},{48,64},{56,72},{64,... | collective-permute-start | bytes 786440 | tf_op jit(solution)/shard_map/ppermute | solution.py:15
  107.8 18.8 %collective-permute-start.14 = (bf16[512,256]{1,0:T(8,128)(2,1)S(1)}, bf16[512,256]{1,0:T(8,128)(2,1)S(1)}, u32[]{:S(2)}, u32[]{:S(2)}) collective-permute-start(bf16[512,256]{1,0:T(8,128)(2,1)S(1)} %pad_maximum_fusion.2), channel_id=1, source_target_pairs={{0,8},{8,16},{16,24},{24,32},{32,40},{40,48},{48,56},{56,64},{64,7... | collective-permute-start | bytes 786440 | tf_op jit(solution)/shard_map/ppermute | solution.py:15
  111.3 15.4 %collective-permute-start.15 = (bf16[512,256]{1,0:T(8,128)(2,1)S(1)}, bf16[512,256]{1,0:T(8,128)(2,1)S(1)}, u32[]{:S(2)}, u32[]{:S(2)}) collective-permute-start(bf16[512,256]{1,0:T(8,128)(2,1)S(1)} %pad_maximum_fusion.2), channel_id=1, source_target_pairs={{8,0},{16,8},{24,16},{32,24},{40,32},{48,40},{56,48},{64,56},{72,6... | collective-permute-start | bytes 786440 | tf_op jit(solution)/shard_map/ppermute | solution.py:15
  116.8 17.4 %collective-permute-start.16 = (bf16[512,256]{1,0:T(8,128)(2,1)S(1)}, bf16[512,256]{1,0:T(8,128)(2,1)S(1)}, u32[]{:S(2)}, u32[]{:S(2)}) collective-permute-start(bf16[512,256]{1,0:T(8,128)(2,1)S(1)} %pad_maximum_fusion.2), channel_id=1, source_target_pairs={{16,0},{24,8},{32,16},{40,24},{48,32},{56,40},{64,48},{72,56},{80,... | collective-permute-start | bytes 786440 | tf_op jit(solution)/shard_map/ppermute | solution.py:15
  120.2 15.6 %collective-permute-start.17 = (bf16[512,256]{1,0:T(8,128)(2,1)S(1)}, bf16[512,256]{1,0:T(8,128)(2,1)S(1)}, u32[]{:S(2)}, u32[]{:S(2)}) collective-permute-start(bf16[512,256]{1,0:T(8,128)(2,1)S(1)} %pad_maximum_fusion.2), channel_id=1, source_target_pairs={{24,0},{32,8},{40,16},{48,24},{56,32},{64,40},{72,48},{80,56},{88,... | collective-permute-start | bytes 786440 | tf_op jit(solution)/shard_map/ppermute | solution.py:15
  138.3 3.3 %copy-start.7 = (bf16[4,12,128,128]{3,2,1,0:T(8,128)(2,1)S(1)}, bf16[4,12,128,128]{3,2,1,0:T(8,128)(2,1)}, u32[]{:S(2)}) copy-start(bf16[4,12,128,128]{3,2,1,0:T(8,128)(2,1)} %param.14) | copy-start | bytes 4718596
  (3 other events, 8.6 us)
where the time goes:
time: 171 us; the launch traced here: 170 us
  starting transfers between devices  68 us (40%)
  blocking collectives  25.8 us (15%)
  waiting for transfers between devices  25.7 us (15%)
  local copies, waits for them, and re-layouts  24.2 us (14%)
  other arithmetic  13.6 us (8%)
  matrix products  10.9 us (6%)
  between operations  1.72 us (1%)
    ppermute x18, starting transfers between devices, from_behind(): lax.ppermute(value, axis, [(source, source + steps) for source in range(l...  68 us
    psum x1, blocking collectives, shards(): scen_total = lax.psum(local_sum, 'scen')  25.8 us
    ppermute x18, waiting for transfers between devices, from_behind(): lax.ppermute(value, axis, [(source, source + steps) for source in range(l...  25.7 us
    unnamed x33, local copies, waits for them, and re-layouts  10.6 us
    gather x3, local copies, waits for them, and re-layouts, shards(): gathered = jnp.take(nearby, window_index, axis=0)  10.5 us
    dot_general x3, matrix products, shards(): jnp.einsum('bsij,bsjk->bik', impedance_real, gathered, preferred_element_...  8.52 us
    scatter-add x1, other arithmetic, shards(): jax.ops.segment_sum(both_power, local_phase, num_segments=phase_count)  6.25 us
  transfers between devices with their start and end apart: 18, of which 5 were waited for; matrix products, arithmetic and copies ran while one was open for 7% of the time, Pallas kernels for 0%

commit v1 on v0

--- a/solution.py
+++ b/solution.py
@@ -83,7 +83,8 @@
         volt_imag = source_imag - drop_imag
     magnitude = jnp.sqrt(volt_real * volt_real + volt_imag * volt_imag)
     local_sum = jnp.sum(magnitude.reshape(phase_count, local_scen, TIMES), axis=1)
-    scen_total = lax.psum(local_sum, "scen")
+    parts = lax.all_gather(local_sum, "scen", axis=0, tiled=False)
+    scen_total = parts.sum(axis=0)
     drop_mean = 100.0 * (1.0 - scen_total / total_scen)
     return (volt_real, volt_imag, drop_mean)
 

time: 171 us -> 160 us (0.936)
  the two profiles are of different devices: /device:TPU:224 before, /device:TPU:195 now
where the time goes in v1:
time: 160 us; the launch traced here: 159 us
  starting transfers between devices  61.1 us (38%)
  waiting for transfers between devices  31.8 us (20%)
  local copies, waits for them, and re-layouts  24.4 us (15%)
  blocking collectives  15.2 us (10%)
  other arithmetic  13.7 us (9%)
  matrix products  10.9 us (7%)
  between operations  1.73 us (1%)
    ppermute x18, starting transfers between devices, from_behind(): lax.ppermute(value, axis, [(source, source + steps) for source in range(l...  61.1 us
    ppermute x18, waiting for transfers between devices, from_behind(): lax.ppermute(value, axis, [(source, source + steps) for source in range(l...  31.8 us
    all_gather x1, blocking collectives, shards(): parts = lax.all_gather(local_sum, 'scen', axis=0, tiled=False)  15.2 us
    unnamed x34, local copies, waits for them, and re-layouts  10.7 us
    gather x3, local copies, waits for them, and re-layouts, shards(): gathered = jnp.take(nearby, window_index, axis=0)  10.5 us
    dot_general x3, matrix products, shards(): jnp.einsum('bsij,bsjk->bik', impedance_real, gathered, preferred_element_...  8.52 us
    scatter-add x1, other arithmetic, shards(): jax.ops.segment_sum(both_power, local_phase, num_segments=phase_count)  6.25 us
  transfers between devices with their start and end apart: 18, of which 6 were waited for; matrix products, arithmetic and copies ran while one was open for 8% of the time, Pallas kernels for 0%

profile of v1, /device:TPU:195, one launch (start us, length us, event | category | flops | bytes accessed | tf_op | source)
XLA Modules:
  0.0 158.8 jit_solution(6651124965556611296)
XLA Ops:
  3.6 6.2 %scatter_custom_fusion = f32[512,256]{1,0:T(8,128)S(1)} fusion(s32[1024]{0:T(1024)S(1)} %broadcast_subtract_fusion, f32[1024,128]{1,0:T(8,128)S(1)} %get-tuple-element.12, f32[]{:T(128)} %constant.112, f32[1024,128]{1,0:T(8,128)S(1)} %get-tuple-element.13, f32[]{:T(128)} %constant.78.clone.1), kind=kCustom, calls=%fused_computation.7 | custom fusion | flops 524288 | bytes 1572872 | tf_op jit(solution)/shard_map/scatter-add | solution.py:44
  10.2 3.5 %collective-permute-start = (bf16[512,256]{1,0:T(8,128)(2,1)S(1)}, bf16[512,256]{1,0:T(8,128)(2,1)}, u32[]{:S(2)}, u32[]{:S(2)}) collective-permute-start(bf16[512,256]{1,0:T(8,128)(2,1)S(1)} %pad_maximum_fusion), channel_id=1, source_target_pairs={{0,24},{8,32},{16,40},{24,48},{32,56},{40,64},{48,72},{56,80},{64,... | collective-permute-start | bytes 786440 | tf_op jit(solution)/shard_map/ppermute | solution.py:15
  13.7 4.0 %collective-permute-start.1 = (bf16[512,256]{1,0:T(8,128)(2,1)S(1)}, bf16[512,256]{1,0:T(8,128)(2,1)}, u32[]{:S(2)}, u32[]{:S(2)}) collective-permute-start(bf16[512,256]{1,0:T(8,128)(2,1)S(1)} %pad_maximum_fusion), channel_id=1, source_target_pairs={{0,16},{8,24},{16,32},{24,40},{32,48},{40,56},{48,64},{56,72},{64,... | collective-permute-start | bytes 786440 | tf_op jit(solution)/shard_map/ppermute | solution.py:15
  17.8 3.4 %collective-permute-start.2 = (bf16[512,256]{1,0:T(8,128)(2,1)S(1)}, bf16[512,256]{1,0:T(8,128)(2,1)S(1)}, u32[]{:S(2)}, u32[]{:S(2)}) collective-permute-start(bf16[512,256]{1,0:T(8,128)(2,1)S(1)} %pad_maximum_fusion), channel_id=1, source_target_pairs={{0,8},{8,16},{16,24},{24,32},{32,40},{40,48},{48,56},{56,64},{64,7... | collective-permute-start | bytes 786440 | tf_op jit(solution)/shard_map/ppermute | solution.py:15
  23.1 3.9 %collective-permute-start.4 = (bf16[512,256]{1,0:T(8,128)(2,1)S(1)}, bf16[512,256]{1,0:T(8,128)(2,1)S(1)}, u32[]{:S(2)}, u32[]{:S(2)}) collective-permute-start(bf16[512,256]{1,0:T(8,128)(2,1)S(1)} %pad_maximum_fusion), channel_id=1, source_target_pairs={{16,0},{24,8},{32,16},{40,24},{48,32},{56,40},{64,48},{72,56},{80,... | collective-permute-start | bytes 786440 | tf_op jit(solution)/shard_map/ppermute | solution.py:15
  29.7 3.5 %collective-permute-start.5 = (bf16[512,256]{1,0:T(8,128)(2,1)S(1)}, bf16[512,256]{1,0:T(8,128)(2,1)S(1)}, u32[]{:S(2)}, u32[]{:S(2)}) collective-permute-start(bf16[512,256]{1,0:T(8,128)(2,1)S(1)} %pad_maximum_fusion), channel_id=1, source_target_pairs={{24,0},{32,8},{40,16},{48,24},{56,32},{64,40},{72,48},{80,56},{88,... | collective-permute-start | bytes 786440 | tf_op jit(solution)/shard_map/ppermute | solution.py:15
  39.5 5.9 %collective-permute-done.5 = bf16[512,256]{1,0:T(8,128)(2,1)S(1)} collective-permute-done((bf16[512,256]{1,0:T(8,128)(2,1)S(1)}, bf16[512,256]{1,0:T(8,128)(2,1)S(1)}, u32[]{:S(2)}, u32[]{:S(2)}) %collective-permute-start.5) | collective-permute-done | bytes 262176 | tf_op jit(solution)/shard_map/ppermute | solution.py:15
  46.2 4.0 %gather_fusion = bf16[48,128,256]{2,1,0:T(8,128)(2,1)} fusion(bf16[28,128,256]{2,1,0:T(8,128)(2,1)} %bitcast.1, s32[1024]{0:T(1024)S(1)} %pad_clamp_fusion), kind=kCustom, calls=%fused_computation.clone | custom fusion | bytes 6291648 | tf_op jit(solution)/shard_map/jit(_take)/gather | solution.py:72
  50.2 2.8 %fusion.4 = f32[4,256,128,1]{1,2,3,0:T(8,128)S(1)} fusion(bf16[4,12,128,128]{3,2,1,0:T(8,128)(2,1)S(1)} %copy-done, bf16[4,12,128,256]{3,2,1,0:T(8,128)(2,1)} %bitcast.58, pred[12]{0:T(512)(128)(4,1)S(1)} %iota_compare_fusion, pred[4,12]{1,0:T(4,128)(4,1)S(1)} %get-tuple-element.10), kind=kOutput, calls=%fused_computation.11 | convolution fusion | flops 405798912 | bytes 5242940 | tf_op jit(solution)/shard_map/bsij,bsjk->bik/dot_general | solution.py:74
  57.4 3.7 %collective-permute-start.7 = (bf16[512,256]{1,0:T(8,128)(2,1)S(1)}, bf16[512,256]{1,0:T(8,128)(2,1)S(1)}, u32[]{:S(2)}, u32[]{:S(2)}) collective-permute-start(bf16[512,256]{1,0:T(8,128)(2,1)S(1)} %pad_maximum_fusion.1), channel_id=1, source_target_pairs={{0,16},{8,24},{16,32},{24,40},{32,48},{40,56},{48,64},{56,72},{64,... | collective-permute-start | bytes 786440 | tf_op jit(solution)/shard_map/ppermute | solution.py:15
  63.0 3.4 %collective-permute-start.9 = (bf16[512,256]{1,0:T(8,128)(2,1)S(1)}, bf16[512,256]{1,0:T(8,128)(2,1)S(1)}, u32[]{:S(2)}, u32[]{:S(2)}) collective-permute-start(bf16[512,256]{1,0:T(8,128)(2,1)S(1)} %pad_maximum_fusion.1), channel_id=1, source_target_pairs={{8,0},{16,8},{24,16},{32,24},{40,32},{48,40},{56,48},{64,56},{72,6... | collective-permute-start | bytes 786440 | tf_op jit(solution)/shard_map/ppermute | solution.py:15
  66.4 4.6 %collective-permute-start.10 = (bf16[512,256]{1,0:T(8,128)(2,1)S(1)}, bf16[512,256]{1,0:T(8,128)(2,1)S(1)}, u32[]{:S(2)}, u32[]{:S(2)}) collective-permute-start(bf16[512,256]{1,0:T(8,128)(2,1)S(1)} %pad_maximum_fusion.1), channel_id=1, source_target_pairs={{16,0},{24,8},{32,16},{40,24},{48,32},{56,40},{64,48},{72,56},{80,... | collective-permute-start | bytes 786440 | tf_op jit(solution)/shard_map/ppermute | solution.py:15
  71.0 4.0 %collective-permute-start.11 = (bf16[512,256]{1,0:T(8,128)(2,1)S(1)}, bf16[512,256]{1,0:T(8,128)(2,1)S(1)}, u32[]{:S(2)}, u32[]{:S(2)}) collective-permute-start(bf16[512,256]{1,0:T(8,128)(2,1)S(1)} %pad_maximum_fusion.1), channel_id=1, source_target_pairs={{24,0},{32,8},{40,16},{48,24},{56,32},{64,40},{72,48},{80,56},{88,... | collective-permute-start | bytes 786440 | tf_op jit(solution)/shard_map/ppermute | solution.py:15
  78.6 3.4 %collective-permute-done.10 = bf16[512,256]{1,0:T(8,128)(2,1)S(1)} collective-permute-done((bf16[512,256]{1,0:T(8,128)(2,1)S(1)}, bf16[512,256]{1,0:T(8,128)(2,1)S(1)}, u32[]{:S(2)}, u32[]{:S(2)}) %collective-permute-start.10) | collective-permute-done | bytes 262176 | tf_op jit(solution)/shard_map/ppermute | solution.py:15
  82.7 6.4 %collective-permute-done.11 = bf16[512,256]{1,0:T(8,128)(2,1)S(1)} collective-permute-done((bf16[512,256]{1,0:T(8,128)(2,1)S(1)}, bf16[512,256]{1,0:T(8,128)(2,1)S(1)}, u32[]{:S(2)}, u32[]{:S(2)}) %collective-permute-start.11) | collective-permute-done | bytes 262176 | tf_op jit(solution)/shard_map/ppermute | solution.py:15
  89.9 4.0 %gather_fusion.1 = bf16[48,128,256]{2,1,0:T(8,128)(2,1)} fusion(bf16[28,128,256]{2,1,0:T(8,128)(2,1)} %bitcast.15, s32[1024]{0:T(1024)S(1)} %pad_clamp_fusion), kind=kCustom, calls=%fused_computation.1.clone | custom fusion | bytes 6291648 | tf_op jit(solution)/shard_map/jit(_take)/gather | solution.py:72
  100.2 3.1 %collective-permute-start.13 = (bf16[512,256]{1,0:T(8,128)(2,1)S(1)}, bf16[512,256]{1,0:T(8,128)(2,1)S(1)}, u32[]{:S(2)}, u32[]{:S(2)}) collective-permute-start(bf16[512,256]{1,0:T(8,128)(2,1)S(1)} %pad_maximum_fusion.2), channel_id=1, source_target_pairs={{0,16},{8,24},{16,32},{24,40},{32,48},{40,56},{48,64},{56,72},{64,... | collective-permute-start | bytes 786440 | tf_op jit(solution)/shard_map/ppermute | solution.py:15
  105.8 3.7 %collective-permute-start.15 = (bf16[512,256]{1,0:T(8,128)(2,1)S(1)}, bf16[512,256]{1,0:T(8,128)(2,1)S(1)}, u32[]{:S(2)}, u32[]{:S(2)}) collective-permute-start(bf16[512,256]{1,0:T(8,128)(2,1)S(1)} %pad_maximum_fusion.2), channel_id=1, source_target_pairs={{8,0},{16,8},{24,16},{32,24},{40,32},{48,40},{56,48},{64,56},{72,6... | collective-permute-start | bytes 786440 | tf_op jit(solution)/shard_map/ppermute | solution.py:15
  109.5 4.6 %collective-permute-start.16 = (bf16[512,256]{1,0:T(8,128)(2,1)S(1)}, bf16[512,256]{1,0:T(8,128)(2,1)S(1)}, u32[]{:S(2)}, u32[]{:S(2)}) collective-permute-start(bf16[512,256]{1,0:T(8,128)(2,1)S(1)} %pad_maximum_fusion.2), channel_id=1, source_target_pairs={{16,0},{24,8},{32,16},{40,24},{48,32},{56,40},{64,48},{72,56},{80,... | collective-permute-start | bytes 786440 | tf_op jit(solution)/shard_map/ppermute | solution.py:15
  114.1 4.6 %collective-permute-start.17 = (bf16[512,256]{1,0:T(8,128)(2,1)S(1)}, bf16[512,256]{1,0:T(8,128)(2,1)S(1)}, u32[]{:S(2)}, u32[]{:S(2)}) collective-permute-start(bf16[512,256]{1,0:T(8,128)(2,1)S(1)} %pad_maximum_fusion.2), channel_id=1, source_target_pairs={{24,0},{32,8},{40,16},{48,24},{56,32},{64,40},{72,48},{80,56},{88,... | collective-permute-start | bytes 786440 | tf_op jit(solution)/shard_map/ppermute | solution.py:15
  118.8 5.6 %collective-permute-done.15 = bf16[512,256]{1,0:T(8,128)(2,1)S(1)} collective-permute-done((bf16[512,256]{1,0:T(8,128)(2,1)S(1)}, bf16[512,256]{1,0:T(8,128)(2,1)S(1)}, u32[]{:S(2)}, u32[]{:S(2)}) %collective-permute-start.15) | collective-permute-done | bytes 262176 | tf_op jit(solution)/shard_map/ppermute | solution.py:15
  124.5 3.5 %collective-permute-done.16 = bf16[512,256]{1,0:T(8,128)(2,1)S(1)} collective-permute-done((bf16[512,256]{1,0:T(8,128)(2,1)S(1)}, bf16[512,256]{1,0:T(8,128)(2,1)S(1)}, u32[]{:S(2)}, u32[]{:S(2)}) %collective-permute-start.16) | collective-permute-done | bytes 262176 | tf_op jit(solution)/shard_map/ppermute | solution.py:15
  128.1 6.9 %collective-permute-done.17 = bf16[512,256]{1,0:T(8,128)(2,1)S(1)} collective-permute-done((bf16[512,256]{1,0:T(8,128)(2,1)S(1)}, bf16[512,256]{1,0:T(8,128)(2,1)S(1)}, u32[]{:S(2)}, u32[]{:S(2)}) %collective-permute-start.17) | collective-permute-done | bytes 262176 | tf_op jit(solution)/shard_map/ppermute | solution.py:15
  142.7 15.2 %all-gather = f32[4096,16]{0,1:T(8,128)S(1)} all-gather(f32[512,16]{0,1:T(8,128)S(1)} %reduce_sum.28), channel_id=2, replica_groups=mesh['net'=64,'scen'=8] {'scen'}, dimensions={0}, use_global_device_ids=true | all-gather | bytes 294912 | tf_op jit(solution)/shard_map/all_gather | solution.py:86
  (85 shorter events, 43.0 us)
Async XLA Ops:
  0.6 49.6 %copy-start = (bf16[4,12,128,128]{3,2,1,0:T(8,128)(2,1)S(1)}, bf16[4,12,128,128]{3,2,1,0:T(8,128)(2,1)}, u32[]{:S(2)}) copy-start(bf16[4,12,128,128]{3,2,1,0:T(8,128)(2,1)} %param.13) | copy-start | bytes 4718596
  3.6 23.5 %copy-start.4 = (s32[4,12]{1,0:T(4,128)S(1)}, s32[4,12]{1,0:T(4,128)}, u32[]{:S(2)}) copy-start(s32[4,12]{1,0:T(4,128)} %param.12) | copy-start | bytes 580
  3.6 23.6 %copy-start.8 = (s32[64]{0:T(128)S(1)}, s32[64]{0:T(128)}, u32[]{:S(2)}) copy-start(s32[64]{0:T(128)} %param.11) | copy-start | bytes 772
  10.2 19.5 %collective-permute-start = (bf16[512,256]{1,0:T(8,128)(2,1)S(1)}, bf16[512,256]{1,0:T(8,128)(2,1)}, u32[]{:S(2)}, u32[]{:S(2)}) collective-permute-start(bf16[512,256]{1,0:T(8,128)(2,1)S(1)} %pad_maximum_fusion), channel_id=1, source_target_pairs={{0,24},{8,32},{16,40},{24,48},{32,56},{40,64},{48,72},{56,80},{64,... | collective-permute-start | bytes 786440 | tf_op jit(solution)/shard_map/ppermute | solution.py:15
  13.7 21.2 %collective-permute-start.1 = (bf16[512,256]{1,0:T(8,128)(2,1)S(1)}, bf16[512,256]{1,0:T(8,128)(2,1)}, u32[]{:S(2)}, u32[]{:S(2)}) collective-permute-start(bf16[512,256]{1,0:T(8,128)(2,1)S(1)} %pad_maximum_fusion), channel_id=1, source_target_pairs={{0,16},{8,24},{16,32},{24,40},{32,48},{40,56},{48,64},{56,72},{64,... | collective-permute-start | bytes 786440 | tf_op jit(solution)/shard_map/ppermute | solution.py:15
  17.8 18.8 %collective-permute-start.2 = (bf16[512,256]{1,0:T(8,128)(2,1)S(1)}, bf16[512,256]{1,0:T(8,128)(2,1)S(1)}, u32[]{:S(2)}, u32[]{:S(2)}) collective-permute-start(bf16[512,256]{1,0:T(8,128)(2,1)S(1)} %pad_maximum_fusion), channel_id=1, source_target_pairs={{0,8},{8,16},{16,24},{24,32},{32,40},{40,48},{48,56},{56,64},{64,7... | collective-permute-start | bytes 786440 | tf_op jit(solution)/shard_map/ppermute | solution.py:15
  21.2 16.8 %collective-permute-start.3 = (bf16[512,256]{1,0:T(8,128)(2,1)S(1)}, bf16[512,256]{1,0:T(8,128)(2,1)S(1)}, u32[]{:S(2)}, u32[]{:S(2)}) collective-permute-start(bf16[512,256]{1,0:T(8,128)(2,1)S(1)} %pad_maximum_fusion), channel_id=1, source_target_pairs={{8,0},{16,8},{24,16},{32,24},{40,32},{48,40},{56,48},{64,56},{72,6... | collective-permute-start | bytes 786440 | tf_op jit(solution)/shard_map/ppermute | solution.py:15
  23.1 15.7 %collective-permute-start.4 = (bf16[512,256]{1,0:T(8,128)(2,1)S(1)}, bf16[512,256]{1,0:T(8,128)(2,1)S(1)}, u32[]{:S(2)}, u32[]{:S(2)}) collective-permute-start(bf16[512,256]{1,0:T(8,128)(2,1)S(1)} %pad_maximum_fusion), channel_id=1, source_target_pairs={{16,0},{24,8},{32,16},{40,24},{48,32},{56,40},{64,48},{72,56},{80,... | collective-permute-start | bytes 786440 | tf_op jit(solution)/shard_map/ppermute | solution.py:15
  29.7 15.7 %collective-permute-start.5 = (bf16[512,256]{1,0:T(8,128)(2,1)S(1)}, bf16[512,256]{1,0:T(8,128)(2,1)S(1)}, u32[]{:S(2)}, u32[]{:S(2)}) collective-permute-start(bf16[512,256]{1,0:T(8,128)(2,1)S(1)} %pad_maximum_fusion), channel_id=1, source_target_pairs={{24,0},{32,8},{40,16},{48,24},{56,32},{64,40},{72,48},{80,56},{88,... | collective-permute-start | bytes 786440 | tf_op jit(solution)/shard_map/ppermute | solution.py:15
  50.2 3.3 %copy-start.5 = (bf16[4,12,128,128]{3,2,1,0:T(8,128)(2,1)S(1)}, bf16[4,12,128,128]{3,2,1,0:T(8,128)(2,1)}, u32[]{:S(2)}) copy-start(bf16[4,12,128,128]{3,2,1,0:T(8,128)(2,1)} %param.14) | copy-start | bytes 4718596
  54.6 16.4 %collective-permute-start.6 = (bf16[512,256]{1,0:T(8,128)(2,1)S(1)}, bf16[512,256]{1,0:T(8,128)(2,1)S(1)}, u32[]{:S(2)}, u32[]{:S(2)}) collective-permute-start(bf16[512,256]{1,0:T(8,128)(2,1)S(1)} %pad_maximum_fusion.1), channel_id=1, source_target_pairs={{0,24},{8,32},{16,40},{24,48},{32,56},{40,64},{48,72},{56,80},{64,... | collective-permute-start | bytes 786440 | tf_op jit(solution)/shard_map/ppermute | solution.py:15
  57.4 18.3 %collective-permute-start.7 = (bf16[512,256]{1,0:T(8,128)(2,1)S(1)}, bf16[512,256]{1,0:T(8,128)(2,1)S(1)}, u32[]{:S(2)}, u32[]{:S(2)}) collective-permute-start(bf16[512,256]{1,0:T(8,128)(2,1)S(1)} %pad_maximum_fusion.1), channel_id=1, source_target_pairs={{0,16},{8,24},{16,32},{24,40},{32,48},{40,56},{48,64},{56,72},{64,... | collective-permute-start | bytes 786440 | tf_op jit(solution)/shard_map/ppermute | solution.py:15
  61.1 15.3 %collective-permute-start.8 = (bf16[512,256]{1,0:T(8,128)(2,1)S(1)}, bf16[512,256]{1,0:T(8,128)(2,1)S(1)}, u32[]{:S(2)}, u32[]{:S(2)}) collective-permute-start(bf16[512,256]{1,0:T(8,128)(2,1)S(1)} %pad_maximum_fusion.1), channel_id=1, source_target_pairs={{0,8},{8,16},{16,24},{24,32},{32,40},{40,48},{48,56},{56,64},{64,7... | collective-permute-start | bytes 786440 | tf_op jit(solution)/shard_map/ppermute | solution.py:15
  63.0 14.9 %collective-permute-start.9 = (bf16[512,256]{1,0:T(8,128)(2,1)S(1)}, bf16[512,256]{1,0:T(8,128)(2,1)S(1)}, u32[]{:S(2)}, u32[]{:S(2)}) collective-permute-start(bf16[512,256]{1,0:T(8,128)(2,1)S(1)} %pad_maximum_fusion.1), channel_id=1, source_target_pairs={{8,0},{16,8},{24,16},{32,24},{40,32},{48,40},{56,48},{64,56},{72,6... | collective-permute-start | bytes 786440 | tf_op jit(solution)/shard_map/ppermute | solution.py:15
  66.4 15.6 %collective-permute-start.10 = (bf16[512,256]{1,0:T(8,128)(2,1)S(1)}, bf16[512,256]{1,0:T(8,128)(2,1)S(1)}, u32[]{:S(2)}, u32[]{:S(2)}) collective-permute-start(bf16[512,256]{1,0:T(8,128)(2,1)S(1)} %pad_maximum_fusion.1), channel_id=1, source_target_pairs={{16,0},{24,8},{32,16},{40,24},{48,32},{56,40},{64,48},{72,56},{80,... | collective-permute-start | bytes 786440 | tf_op jit(solution)/shard_map/ppermute | solution.py:15
  71.0 18.2 %collective-permute-start.11 = (bf16[512,256]{1,0:T(8,128)(2,1)S(1)}, bf16[512,256]{1,0:T(8,128)(2,1)S(1)}, u32[]{:S(2)}, u32[]{:S(2)}) collective-permute-start(bf16[512,256]{1,0:T(8,128)(2,1)S(1)} %pad_maximum_fusion.1), channel_id=1, source_target_pairs={{24,0},{32,8},{40,16},{48,24},{56,32},{64,40},{72,48},{80,56},{88,... | collective-permute-start | bytes 786440 | tf_op jit(solution)/shard_map/ppermute | solution.py:15
  93.9 3.3 %copy-start.6 = (bf16[4,12,128,128]{3,2,1,0:T(8,128)(2,1)S(1)}, bf16[4,12,128,128]{3,2,1,0:T(8,128)(2,1)}, u32[]{:S(2)}) copy-start(bf16[4,12,128,128]{3,2,1,0:T(8,128)(2,1)} %param.14) | copy-start | bytes 4718596
  98.3 15.8 %collective-permute-start.12 = (bf16[512,256]{1,0:T(8,128)(2,1)S(1)}, bf16[512,256]{1,0:T(8,128)(2,1)S(1)}, u32[]{:S(2)}, u32[]{:S(2)}) collective-permute-start(bf16[512,256]{1,0:T(8,128)(2,1)S(1)} %pad_maximum_fusion.2), channel_id=1, source_target_pairs={{0,24},{8,32},{16,40},{24,48},{32,56},{40,64},{48,72},{56,80},{64,... | collective-permute-start | bytes 786440 | tf_op jit(solution)/shard_map/ppermute | solution.py:15
  100.2 18.5 %collective-permute-start.13 = (bf16[512,256]{1,0:T(8,128)(2,1)S(1)}, bf16[512,256]{1,0:T(8,128)(2,1)S(1)}, u32[]{:S(2)}, u32[]{:S(2)}) collective-permute-start(bf16[512,256]{1,0:T(8,128)(2,1)S(1)} %pad_maximum_fusion.2), channel_id=1, source_target_pairs={{0,16},{8,24},{16,32},{24,40},{32,48},{40,56},{48,64},{56,72},{64,... | collective-permute-start | bytes 786440 | tf_op jit(solution)/shard_map/ppermute | solution.py:15
  103.3 15.5 %collective-permute-start.14 = (bf16[512,256]{1,0:T(8,128)(2,1)S(1)}, bf16[512,256]{1,0:T(8,128)(2,1)S(1)}, u32[]{:S(2)}, u32[]{:S(2)}) collective-permute-start(bf16[512,256]{1,0:T(8,128)(2,1)S(1)} %pad_maximum_fusion.2), channel_id=1, source_target_pairs={{0,8},{8,16},{16,24},{24,32},{32,40},{40,48},{48,56},{56,64},{64,7... | collective-permute-start | bytes 786440 | tf_op jit(solution)/shard_map/ppermute | solution.py:15
  105.8 18.7 %collective-permute-start.15 = (bf16[512,256]{1,0:T(8,128)(2,1)S(1)}, bf16[512,256]{1,0:T(8,128)(2,1)S(1)}, u32[]{:S(2)}, u32[]{:S(2)}) collective-permute-start(bf16[512,256]{1,0:T(8,128)(2,1)S(1)} %pad_maximum_fusion.2), channel_id=1, source_target_pairs={{8,0},{16,8},{24,16},{32,24},{40,32},{48,40},{56,48},{64,56},{72,6... | collective-permute-start | bytes 786440 | tf_op jit(solution)/shard_map/ppermute | solution.py:15
  109.5 18.6 %collective-permute-start.16 = (bf16[512,256]{1,0:T(8,128)(2,1)S(1)}, bf16[512,256]{1,0:T(8,128)(2,1)S(1)}, u32[]{:S(2)}, u32[]{:S(2)}) collective-permute-start(bf16[512,256]{1,0:T(8,128)(2,1)S(1)} %pad_maximum_fusion.2), channel_id=1, source_target_pairs={{16,0},{24,8},{32,16},{40,24},{48,32},{56,40},{64,48},{72,56},{80,... | collective-permute-start | bytes 786440 | tf_op jit(solution)/shard_map/ppermute | solution.py:15
  114.1 20.8 %collective-permute-start.17 = (bf16[512,256]{1,0:T(8,128)(2,1)S(1)}, bf16[512,256]{1,0:T(8,128)(2,1)S(1)}, u32[]{:S(2)}, u32[]{:S(2)}) collective-permute-start(bf16[512,256]{1,0:T(8,128)(2,1)S(1)} %pad_maximum_fusion.2), channel_id=1, source_target_pairs={{24,0},{32,8},{40,16},{48,24},{56,32},{64,40},{72,48},{80,56},{88,... | collective-permute-start | bytes 786440 | tf_op jit(solution)/shard_map/ppermute | solution.py:15
  137.4 3.3 %copy-start.7 = (bf16[4,12,128,128]{3,2,1,0:T(8,128)(2,1)S(1)}, bf16[4,12,128,128]{3,2,1,0:T(8,128)(2,1)}, u32[]{:S(2)}) copy-start(bf16[4,12,128,128]{3,2,1,0:T(8,128)(2,1)} %param.14) | copy-start | bytes 4718596
  (3 other events, 8.6 us)
